TPU v7x, 32 devices: a whole 2x2x4 slice. The times are simulated.
32 devices in a mesh: grp: 2 (over x), lon: 16 (over z, y, core).
Axes of the slice: x: 2, y: 2, z: 4, core: 2. Of those that a mesh axis runs over, the one named last changes fastest.
Arguments:
- tracers: float32 [64, 4, 96, 256], P('grp', None, 'lon'), parts along dimension 0, may hold values from -6 to 6
- air_mass: float32 [4, 96, 256], P(None, None, 'lon'), may hold values from 1 to 2
- east_flux: float32 [4, 96, 256], P(None, None, 'lon'), may hold values from -0.24 to 0.24, as said below
- north_flux: float32 [4, 96, 256], P(None, None, 'lon'), may hold values from -0.025 to 0.025, as said below
- south_flux: float32 [4, 96], replicated, may hold values from -0.025 to 0.025, as said below
- upward_flux: float32 [3, 96, 256], P(None, None, 'lon'), may hold values from -0.025 to 0.025
- emission: float32 [96, 256], P('lon'), may hold values from 0.5 to 2
- region_map: int32 [96, 256], P('lon'), may hold values from 0 to 31
- limiter_flags: int32 [6], replicated, may hold values 0 or 1
- substep_counts: int32 [256], replicated, may hold values from 1 to 3, as said below
Outputs:
- transported: float32 [64, 4, 96, 256], P('grp', None, 'lon'), parts along dimension 0
- final_mass: float32 [8, 96, 256], P('grp', 'lon'), parts along dimension 0
There are 2 independent parts, one for each index of `grp`. A program takes and returns all parts, laid end to end along the dimension named above; an argument that names none is the same for every part. Nothing has to cross between parts.
Inputs may be any that keep to these rules, and one draw needn't show every extreme that they name: `substep_counts`: the 32 rows nearest each pole have 3 substeps. `east_flux`: the magnitude is at most 0.08 times the substep count of the row. `north_flux`: in the last latitude row (the north pole face) the flux at a longitude is minus the flux 96 / 2 cells away. `south_flux`: the flux at a longitude is minus the flux 96 / 2 cells away.
All inputs are finite; a program needn't handle non-finite values.
Results may differ from a plain program's by a relative error of at most 0.0003.
Values sent between devices are 32-bit elements; how exact they have to be, the bound alone decides.
A program may use at most 64 MiB of HBM per device.

v0:
```python
import functools

import jax
import jax.numpy as jnp
from jax import lax
from jax.experimental import pallas as pl
from jax.experimental.pallas import tpu as pltpu
from jax.sharding import PartitionSpec as P

MAXSUB = 3
ROWS = 8
LANES = 128
FIELDS = 16


def minmod(a, b):
    return jnp.maximum(jnp.minimum(a, b), 0.0) + jnp.minimum(jnp.maximum(a, b), 0.0)


def kernel(
    devices,
    levels,
    columns,
    chunks,
    tin,
    spack,
    south,
    scal,
    out,
    mass_out,
    recv,
    field,
    mass,
    inv,
    fx,
    cx,
    fy,
    cy,
    cz,
    hl1,
    hr1,
    hl2,
    hr2,
    state,
    mpack,
    mopp,
    coefs,
    ppack,
    popp,
    f_send,
    f_recv,
    h_send,
    h_recv,
    p_send,
    p_recv,
    m_sem,
):
    me = lax.axis_index("lon")
    right = lax.rem(me + 1, devices)
    left = lax.rem(me + devices - 1, devices)
    opposite = lax.rem(me + devices // 2, devices)
    cells = levels * columns
    lat = tin.shape[-1]
    lat_b = lat // devices
    per_row = LANES // lat_b
    wide = 3 * columns

    def remote(src, dst, send, recv_, to):
        return pltpu.make_async_remote_copy(
            src_ref=src,
            dst_ref=dst,
            send_sem=send,
            recv_sem=recv_,
            device_id={"lon": to},
            device_id_type=pl.DeviceIdType.MESH,
        )

    barrier = pltpu.get_barrier_semaphore()
    for off in range(1, devices):
        pl.semaphore_signal(
            barrier,
            inc=1,
            device_id={"lon": lax.rem(me + off, devices)},
            device_id_type=pl.DeviceIdType.MESH,
        )
    pl.semaphore_wait(barrier, devices - 1)

    def field_copy(off):
        to = lax.rem(me + off, devices)
        return remote(spack.at[to], recv.at[me], f_send.at[off], f_recv.at[off], to)

    def field_wait(off):
        source = lax.rem(me + devices - off, devices)
        return remote(spack.at[source], recv.at[source], f_send.at[off], f_recv.at[off], source)

    for off in range(1, devices):
        field_copy(off).start()

    def to_right(ch, phase):
        src, dst = (tin, hl1) if phase == 0 else (state, hl2)
        return remote(
            src.at[ch], dst.at[ch], h_send.at[phase, 0, ch], h_recv.at[phase, 0, ch], right
        )

    def to_left(ch, phase):
        src, dst = (tin, hr1) if phase == 0 else (state, hr2)
        return remote(
            src.at[ch], dst.at[ch], h_send.at[phase, 1, ch], h_recv.at[phase, 1, ch], left
        )

    for ch in range(chunks):
        to_right(ch, 0).start()
        to_left(ch, 0).start()

    recv[me] = spack[me]
    for off in range(1, devices):
        field_wait(off).wait_recv()

    lane = lax.broadcasted_iota(jnp.int32, (1, LANES), 1)
    lane_lat = lax.broadcasted_iota(jnp.int32, (1, lat), 1)
    first = lane_lat == 0
    final = lane_lat == lat - 1

    for h in range(FIELDS // per_row):

        def unpack(g, carry, h=h):
            for half in range(lat // LANES):
                acc = jnp.zeros((recv.shape[2], LANES), jnp.float32)
                for place in range(per_row):
                    piece = recv[half * per_row + place, h]
                    turned = pltpu.roll(
                        piece, lax.rem(lat_b * (place + per_row - g), LANES), 1
                    )
                    acc = jnp.where(lane // lat_b == place, turned, acc)
                field[g * (FIELDS // per_row) + h, :, half * LANES : (half + 1) * LANES] = acc
            return carry

        lax.fori_loop(0, per_row, unpack, 0)

    def half_switch(number):
        return 0.5 * scal[MAXSUB + number : MAXSUB + number + 1, :]

    def second_order(flux, inv_up, number):
        size = jnp.abs(flux)
        return half_switch(number) * size * (1.0 - size * inv_up)

    tall = field.shape[1]

    def x_air(l, base, number):
        m = mass[base, l]
        r = inv[base, l]
        for k in range(MAXSUB):
            flux = fx[k, l]
            r_next = pltpu.roll(r, tall - 1, 0)
            slot = k if base == 0 else MAXSUB + k
            cx[slot, l] = second_order(flux, jnp.where(flux >= 0.0, r, r_next), number)
            m = m - (flux - pltpu.roll(flux, 1, 0))
            r = 1.0 / m
            mass[base + k + 1, l] = m
            inv[base + k + 1, l] = r

    def y_air(l, base, number, slot):
        m = mass[base, l]
        r = inv[base, l]
        flux = fy[l]
        r_low = pltpu.roll(r, 1, 1)
        cy[slot, l] = second_order(flux, jnp.where(flux >= 0.0, r_low, r), number)
        upper = jnp.where(final, field[2 * levels + l], pltpu.roll(flux, lat - 1, 1))
        m = m - (upper - flux)
        mass[base + 1, l] = m
        inv[base + 1, l] = 1.0 / m

    def z_air(base, number, slot):
        lower = 0.0
        for l in range(levels):
            m = mass[base, l]
            if l < levels - 1:
                upper = field[3 * levels + l]
                cz[slot, l] = second_order(
                    upper, jnp.where(upper >= 0.0, inv[base, l], inv[base, l + 1]), number
                )
                m = m - (upper - lower)
            else:
                m = m + lower
            lower = upper
            mass[base + 1, l] = m
            inv[base + 1, l] = 1.0 / m

    def air_first(l, carry):
        m = field[l]
        mass[0, l] = m
        inv[0, l] = 1.0 / m
        east = field[levels + l]
        for k in range(MAXSUB):
            fx[k, l] = east * scal[k : k + 1, :]
        north = field[2 * levels + l]
        fy[l] = jnp.where(first, south[l], pltpu.roll(north, 1, 1))
        x_air(l, 0, 0)
        y_air(l, 3, 1, 0)
        return carry

    def air_last(l, carry):
        y_air(l, 6, 4, 1)
        x_air(l, 7, 5)
        mass_out[l] = mass[10, l, columns : 2 * columns, :]
        return carry

    lax.fori_loop(0, levels, air_first, 0)
    z_air(4, 2, 0)
    z_air(5, 3, 1)
    lax.fori_loop(0, levels, air_last, 0)

    def place_poles(values, cell, acc):
        ends = jnp.where(lane < LANES // 2, values[:, :LANES], values[:, lat - LANES :])
        ends = jnp.broadcast_to(ends, (ROWS, LANES))
        turned = pltpu.roll(ends, 4 * cell + 2, 1)
        return jnp.where(lane // 4 == cell, turned, acc)

    def air_poles(l, carry):
        accs = list(carry)
        for j in range(columns):
            cell = l * columns + j
            c = columns + j
            accs[0] = place_poles(mass[3, l, c : c + 1, :], cell, accs[0])
            accs[1] = place_poles(mass[6, l, c : c + 1, :], cell, accs[1])
            inflow = jnp.where(
                first, fy[l, c : c + 1, :], -field[2 * levels + l, c : c + 1, :]
            )
            accs[2] = place_poles(inflow, cell, accs[2])
        return tuple(accs)

    nothing = jnp.zeros((ROWS, LANES), jnp.float32)
    packs = lax.fori_loop(0, levels, air_poles, (nothing + 1.0, nothing + 1.0, nothing))
    mpack[0] = packs[0]
    mpack[1] = packs[1]
    inflow = packs[2]
    masses_away = remote(mpack, mopp, m_sem.at[0], m_sem.at[1], opposite)
    masses_away.start()
    masses_away.wait_recv()
    for turn, number in ((0, 1), (1, 4)):
        up = jnp.where(inflow >= 0.0, mopp[turn], mpack[turn])
        size = jnp.abs(inflow)
        coefs[turn] = half_switch(number)[:, :LANES] * size * (1.0 - size / up)
    coefs[2] = inflow

    def row(ref, index, l, c):
        return ref[index, l, c : c + 1, :]

    def x_sub(q, lo, hi, base, slot, k, l, keep):
        jump = {c: q[c] - q[c - 1] for c in range(lo + 1, hi + 1)}
        slope = {c: minmod(jump[c], jump[c + 1]) for c in range(lo + 1, hi)}
        carried = {}
        for c in range(lo + 1, hi - 1):
            flux = row(fx, k, l, c)
            ahead = jnp.broadcast_to(flux, (ROWS, lat)) >= 0.0
            carried[c] = flux * jnp.where(ahead, q[c], q[c + 1]) + row(cx, slot, l, c) * jnp.where(
                ahead, slope[c], slope[c + 1]
            )
        fresh = {}
        for c in range(lo + 2, hi - 1):
            t = row(mass, base, l, c) * q[c] - (carried[c] - carried[c - 1])
            fresh[c] = t if keep else t * row(inv, base + 1, l, c)
        return fresh

    def x_three(q, l, base, slot, keep):
        for k in range(MAXSUB):
            q = x_sub(
                q,
                2 * k,
                wide - 1 - 2 * k,
                base + k,
                slot + k,
                k,
                l,
                keep and k == MAXSUB - 1,
            )
        return q

    def stage_a(ch):
        to_right(ch, 0).wait_recv()
        to_left(ch, 0).wait_recv()

        def level(l, acc):
            q = {}
            for c in range(wide):
                source = (hl1, tin, hr1)[c // columns]
                q[c] = source[ch, l * columns + c % columns] * row(inv, 0, l, c)
            q = x_three(q, l, 0, 0, False)
            for j in range(columns):
                state[ch, l * columns + j] = q[columns + j]
                acc = place_poles(q[columns + j], l * columns + j, acc)
            return acc

        ppack[0, ch] = lax.fori_loop(0, levels, level, nothing)
        poles(ch, 0).start()

    def poles(ch, turn):
        return remote(
            ppack.at[turn, ch],
            popp.at[turn, ch],
            p_send.at[turn, ch],
            p_recv.at[turn, ch],
            opposite,
        )

    def polar(ch, turn):
        poles(ch, turn).wait_recv()
        mine = ppack[turn, ch]
        other = popp[turn, ch]

        def inner(x):
            return jnp.where(lane % 4 == 1, pltpu.roll(x, 1, 1), pltpu.roll(x, LANES - 1, 1))

        across = mine - other
        slope_mine = minmod(across, inner(mine) - mine)
        slope_other = minmod(across, other - inner(other))
        inflow = coefs[2]
        entering = inflow >= 0.0
        carried = inflow * jnp.where(entering, other, mine) + coefs[turn] * jnp.where(
            entering, slope_other, slope_mine
        )
        return across, carried

    def y_level(ch, turn, base, across, carried, l):
        results = []
        for j in range(columns):
            cell = l * columns + j
            back = LANES - 2 - 4 * cell
            edge = pltpu.roll(across, back, 1)
            edge = jnp.concatenate([edge] * (lat // LANES), axis=1)
            enter = pltpu.roll(carried, back, 1)
            enter = jnp.concatenate([enter] * (lat // LANES), axis=1)
            c = columns + j
            q = state[ch, cell]
            low = pltpu.roll(q, 1, 1)
            jump = jnp.where(first, edge, q - low)
            slope = minmod(jump, jnp.where(final, -edge, pltpu.roll(jump, lat - 1, 1)))
            flux = fy[l, c : c + 1, :]
            ahead = jnp.broadcast_to(flux, (ROWS, lat)) >= 0.0
            through = flux * jnp.where(ahead, low, q) + row(cy, turn, l, c) * jnp.where(
                ahead, pltpu.roll(slope, 1, 1), slope
            )
            through = jnp.where(first, enter, through)
            above = jnp.where(final, -enter, pltpu.roll(through, lat - 1, 1))
            results.append(
                (row(mass, base, l, c) * q - (above - through)) * row(inv, base + 1, l, c)
            )
        for j in range(columns):
            state[ch, l * columns + j] = results[j]

    def stage_b(ch):
        across, carried = polar(ch, 0)

        def level(l, carry):
            y_level(ch, 0, 3, across, carried, l)
            return carry

        lax.fori_loop(0, levels, level, 0)
        acc = nothing
        for j in range(columns):
            c = columns + j
            q = [state[ch, l * columns + j] for l in range(levels)]
            for turn in range(2):
                jump = [q[l + 1] - q[l] for l in range(levels - 1)]
                zero = jnp.zeros_like(q[0])
                slope = (
                    [zero]
                    + [minmod(jump[l - 1], jump[l]) for l in range(1, levels - 1)]
                    + [zero]
                )
                carried_up = []
                for l in range(levels - 1):
                    flux = field[3 * levels + l, c : c + 1, :]
                    ahead = jnp.broadcast_to(flux, (ROWS, lat)) >= 0.0
                    carried_up.append(
                        flux * jnp.where(ahead, q[l], q[l + 1])
                        + row(cz, turn, l, c) * jnp.where(ahead, slope[l], slope[l + 1])
                    )
                fresh = []
                for l in range(levels):
                    t = row(mass, 4 + turn, l, c) * q[l]
                    if l < levels - 1:
                        t = t - carried_up[l]
                    if l > 0:
                        t = t + carried_up[l - 1]
                    fresh.append(t * row(inv, 5 + turn, l, c))
                q = fresh
            for l in range(levels):
                state[ch, l * columns + j] = q[l]
                acc = place_poles(q[l], l * columns + j, acc)
        ppack[1, ch] = acc
        poles(ch, 1).start()

    def stage_c(ch):
        across, carried = polar(ch, 1)

        def level(l, carry):
            y_level(ch, 1, 6, across, carried, l)
            return carry

        lax.fori_loop(0, levels, level, 0)
        to_right(ch, 1).start()
        to_left(ch, 1).start()

    def step(i, carry):
        @pl.when(i < chunks)
        def _():
            stage_a(i)

        @pl.when((i >= 1) & (i < chunks + 1))
        def _():
            stage_b(i - 1)

        @pl.when(i >= 2)
        def _():
            stage_c(i - 2)

        return carry

    lax.fori_loop(0, chunks + 2, step, 0)

    def stage_d(ch, carry):
        to_right(ch, 1).wait_recv()
        to_left(ch, 1).wait_recv()

        def level(l, carry):
            q = {}
            for c in range(wide):
                source = (hl2, state, hr2)[c // columns]
                q[c] = source[ch, l * columns + c % columns]
            q = x_three(q, l, 7, MAXSUB, True)
            for j in range(columns):
                out[ch, l * columns + j] = q[columns + j]
            return carry

        lax.fori_loop(0, levels, level, 0)
        return carry

    lax.fori_loop(0, chunks, stage_d, 0)

    for off in range(1, devices):
        field_copy(off).wait_send()
    for ch in range(chunks):
        for phase in range(2):
            to_right(ch, phase).wait_send()
            to_left(ch, phase).wait_send()
            poles(ch, phase).wait_send()
    masses_away.wait_send()


def per_device(
    tracers,
    air_mass,
    east_flux,
    north_flux,
    south_flux,
    upward_flux,
    emission,
    region_map,
    limiter_flags,
    substep_counts,
):
    devices = lax.axis_size("lon")
    position = lax.axis_index("lon")
    count, levels, columns, lat = tracers.shape
    chunks = count // ROWS
    cells = levels * columns
    lat_b = lat // devices
    per_row = LANES // lat_b
    folds = FIELDS // per_row
    tall = -(-3 * columns // 8) * 8

    labels = jnp.arange(count, dtype=jnp.int32)
    tagged = (region_map[None] == labels[:, None, None]).astype(jnp.float32)
    surface = tracers[:, 0] + emission[None] * tagged
    seeded = jnp.concatenate([surface[:, None], tracers[:, 1:]], axis=1)
    tin = seeded.reshape(chunks, ROWS, cells, lat).transpose(0, 2, 1, 3)

    fields = jnp.concatenate([air_mass, east_flux, north_flux, upward_flux], axis=0)
    fields = jnp.pad(fields, ((0, FIELDS - fields.shape[0]), (0, 0), (0, 0)))
    bands = fields.reshape(per_row, folds, devices, columns, lat_b)
    bands = bands.transpose(2, 1, 3, 0, 4).reshape(devices, folds, columns, LANES)
    spack = jnp.concatenate([jnp.roll(bands, 1, 0), bands, jnp.roll(bands, -1, 0)], axis=2)
    spack = jnp.pad(spack, ((0, 0), (0, 0), (0, tall - 3 * columns), (0, 0)))

    doubled = jnp.concatenate([south_flux[:, -columns:], south_flux, south_flux[:, :tall]], axis=1)
    south = lax.dynamic_slice_in_dim(doubled, position * columns, tall, 1)[:, :, None]

    counts = substep_counts.astype(jnp.float32)
    scal = jnp.concatenate(
        [
            jnp.where(
                jnp.arange(MAXSUB)[:, None] < substep_counts[None], 1.0 / counts[None], 0.0
            ),
            jnp.broadcast_to(limiter_flags.astype(jnp.float32)[:, None], (6, lat)),
        ],
        axis=0,
    )

    vmem = functools.partial(pltpu.VMEM, dtype=jnp.float32)
    band = (chunks, cells, ROWS, lat)
    dma = pltpu.SemaphoreType.DMA
    out, final_mass = pl.pallas_call(
        functools.partial(kernel, devices, levels, columns, chunks),
        out_shape=(
            jax.ShapeDtypeStruct(band, jnp.float32),
            jax.ShapeDtypeStruct((levels, columns, lat), jnp.float32),
        ),
        in_specs=[pl.BlockSpec(memory_space=pltpu.VMEM)] * 4,
        out_specs=[pl.BlockSpec(memory_space=pltpu.VMEM)] * 2,
        scratch_shapes=[
            vmem((devices, folds, tall, LANES)),
            vmem((FIELDS, tall, lat)),
            vmem((11, levels, tall, lat)),
            vmem((11, levels, tall, lat)),
            vmem((MAXSUB, levels, tall, lat)),
            vmem((2 * MAXSUB, levels, tall, lat)),
            vmem((levels, tall, lat)),
            vmem((2, levels, tall, lat)),
            vmem((2, levels, tall, lat)),
            vmem(band),
            vmem(band),
            vmem(band),
            vmem(band),
            vmem(band),
            vmem((2, ROWS, LANES)),
            vmem((2, ROWS, LANES)),
            vmem((3, ROWS, LANES)),
            vmem((2, chunks, ROWS, LANES)),
            vmem((2, chunks, ROWS, LANES)),
            dma((devices,)),
            dma((devices,)),
            dma((2, 2, chunks)),
            dma((2, 2, chunks)),
            dma((2, chunks)),
            dma((2, chunks)),
            dma((2,)),
        ],
        compiler_params=pltpu.CompilerParams(
            collective_id=0, has_side_effects=True, vmem_limit_bytes=40 * 2**20
        ),
    )(tin, spack, south, scal)
    transported = (
        out.reshape(chunks, cells, ROWS, lat)
        .transpose(0, 2, 1, 3)
        .reshape(count, levels, columns, lat)
    )
    return transported, final_mass


def solution(mesh):
    return jax.shard_map(
        per_device,
        mesh=mesh,
        in_specs=(
            P("grp", None, "lon", None),
            P(None, None, "lon"),
            P(None, None, "lon"),
            P(None, None, "lon"),
            P(),
            P(None, None, "lon"),
            P("lon", None),
            P("lon", None),
            P(),
            P(),
        ),
        out_specs=(P("grp", None, "lon", None), P("grp", "lon", None)),
        check_vma=False,
    )
```

profile of v0, /device:TPU:1, one launch (start us, length us, event | category | flops | bytes accessed | tf_op | source)
XLA Modules:
  0.0 66.6 jit_solution(3824798734369563767)
XLA Ops:
  0.6 0.0 copy-start.8
  0.6 0.0 copy-start.7
  0.7 0.6 copy-done.8
  1.3 0.0 copy-start.4
  1.3 0.0 copy-start.3
  1.3 0.1 pad.11.clone
  1.4 0.0 copy-done.7
  1.4 0.6 copy-done.4
  2.0 0.1 slice.50
  2.0 0.1 pad_maximum_fusion.3
  2.1 0.1 dynamic-slice_bitcast_fusion
  2.2 0.0 copy-start.1
  2.2 0.0 copy-start.2
  2.2 0.1 pad_maximum_fusion.2.scal
  2.3 0.1 copy.50.south
  2.4 0.0 copy-done.3
  2.4 0.6 copy-done.1
  3.0 0.0 copy-done.2
  3.0 0.7 %pad_maximum_fusion.1 = f32[15,96,16]{1,2,0:T(8,128)S(1)} fusion(f32[3,96,16]{1,2,0:T(8,128)} %param.15, f32[4,96,16]{1,2,0:T(8,128)S(1)} %copy-done.1, f32[4,96,16]{1,2,0:T(8,128)S(1)} %copy-done.2, f32[4,96,16]{1,2,0:T(8,128)S(1)} %copy-done.3), kind=kLoop, calls=%fused_computation.9 | loop fusion | flops 69120 | bytes 184320 | tf_op jit(solution)/shard_map/concatenate | solution.py:479
  3.7 0.0 slice-start
  3.7 0.0 copy-start.5
  3.8 0.0 copy-start.6
  3.8 0.9 %slice-done = f32[32,1,6,256]{3,1,2,0:T(1,128)S(1)} async-done(((f32[32,4,6,256]{3,1,2,0:T(4,128)}), f32[32,1,6,256]{3,1,2,0:T(1,128)S(1)}, s32[]{:S(2)}) %slice-start) | async-done | bytes 196632 | tf_op jit(solution)/shard_map/slice | solution.py:475
  4.7 0.0 copy-done.5
  4.7 0.0 copy-done.6
  4.7 0.4 copy.39
  5.1 0.1 pad.8
  5.2 0.1 reshape.39
  5.3 0.1 reshape.43
  5.4 0.1 copy.56
  5.4 0.2 reshape.41
  5.7 0.4 fusion.3
  6.1 0.2 reshape.40
  6.4 0.0 copy-start
  6.5 0.2 reshape.42
  6.7 0.1 fusion.spack
  6.8 0.8 %copy-done = f32[32,4,6,256]{3,1,2,0:T(4,128)S(1)} copy-done((f32[32,4,6,256]{3,1,2,0:T(4,128)S(1)}, f32[32,4,6,256]{3,1,2,0:T(4,128)}, u32[]{:S(2)}) %copy-start) | copy-done | bytes 786456
  7.6 0.2 slice.41
  7.8 0.2 copy.65
  8.0 0.1 pad_maximum_fusion
  8.1 0.1 copy.68
  8.1 56.3 %shard_map.113 = (f32[4,24,8,256]{3,2,1,0:T(8,128)S(1)}, f32[4,6,256]{2,1,0:T(8,128)S(1)}) custom-call(f32[4,24,8,256]{3,2,1,0:T(8,128)S(1)} %bitcast.22, f32[16,2,24,128]{3,2,1,0:T(8,128)S(1)} %fusion.spack, f32[4,24,1]{2,1,0:T(8,128)S(1)} %copy.50.south, f32[9,256]{1,0:T(8,128)S(1)} %pad_maximum_fusion.2.scal), custom_call_target="tpu_custom_call" | custom-call | tf_op jit(solution)/shard_map/pallas_call | solution.py:503
  64.5 0.1 copy.51
  64.6 1.4 %copy.52 = f32[32,4,6,256]{3,1,2,0:T(4,128)} copy(f32[32,4,6,256]{3,0,2,1:T(8,128)S(1)} %bitcast.28) | data formatting | bytes 1572864
  66.0 0.6 copy.53
  (9 shorter events, 0.2 us)
Async XLA Ops:
  0.6 0.7 copy-start.8
  0.6 0.7 %copy-start.7 = (s32[256]{0:T(256)S(1)}, s32[256]{0:T(256)}, u32[]{:S(2)}) copy-start(s32[256]{0:T(256)} %param.19) | copy-start | bytes 3076
  1.3 0.7 %copy-start.4 = (f32[4,96]{1,0:T(4,128)S(1)}, f32[4,96]{1,0:T(4,128)}, u32[]{:S(2)}) copy-start(f32[4,96]{1,0:T(4,128)} %param.14) | copy-start | bytes 4612
  1.3 1.1 %copy-start.3 = (f32[4,96,16]{1,2,0:T(8,128)S(1)}, f32[4,96,16]{1,2,0:T(8,128)}, u32[]{:S(2)}) copy-start(f32[4,96,16]{1,2,0:T(8,128)} %param.11) | copy-start | bytes 73732
  2.2 0.8 %copy-start.1 = (f32[4,96,16]{1,2,0:T(8,128)S(1)}, f32[4,96,16]{1,2,0:T(8,128)}, u32[]{:S(2)}) copy-start(f32[4,96,16]{1,2,0:T(8,128)} %param.13) | copy-start | bytes 73732
  2.2 0.8 %copy-start.2 = (f32[4,96,16]{1,2,0:T(8,128)S(1)}, f32[4,96,16]{1,2,0:T(8,128)}, u32[]{:S(2)}) copy-start(f32[4,96,16]{1,2,0:T(8,128)} %param.12) | copy-start | bytes 73732
  3.7 0.9 %slice-start = ((f32[32,4,6,256]{3,1,2,0:T(4,128)}), f32[32,1,6,256]{3,1,2,0:T(1,128)S(1)}, s32[]{:S(2)}) async-start(f32[32,4,6,256]{3,1,2,0:T(4,128)} %param.10), calls=%async_computation | async-start | bytes 393216 | tf_op jit(solution)/shard_map/slice | solution.py:475
  3.7 0.9 %copy-start.5 = (f32[6,256]{1,0:T(8,128)S(1)}, f32[6,256]{1,0:T(8,128)}, u32[]{:S(2)}) copy-start(f32[6,256]{1,0:T(8,128)} %param.16) | copy-start | bytes 18436
  3.8 0.9 %copy-start.6 = (s32[6,256]{1,0:T(8,128)S(1)}, s32[6,256]{1,0:T(8,128)}, u32[]{:S(2)}) copy-start(s32[6,256]{1,0:T(8,128)} %param.17) | copy-start | bytes 18436
  6.4 1.1 %copy-start = (f32[32,4,6,256]{3,1,2,0:T(4,128)S(1)}, f32[32,4,6,256]{3,1,2,0:T(4,128)}, u32[]{:S(2)}) copy-start(f32[32,4,6,256]{3,1,2,0:T(4,128)} %param.10) | copy-start | bytes 2359300
where the time goes:
time: 67 us; the launch traced here: 66.6 us
  Pallas kernels  56.3 us (84%)
  local copies, waits for them, and re-layouts  8.32 us (12%)
  other arithmetic  1.08 us (2%)
  between operations  0.86 us (1%)
    pallas_call x1, Pallas kernels, per_device(): pl.pallas_call(functools.partial(kernel, devices, levels, columns, chunks...  56.3 us
    unnamed x21, local copies, waits for them, and re-layouts  4.85 us

commit v1 on v0

--- a/solution.py
+++ b/solution.py
@@ -23,11 +23,20 @@
     columns,
     chunks,
     tin,
+    air_in,
+    east_in,
+    north_in,
+    up_in,
+    south_in,
+    counts_in,
+    flags_in,
+    out,
+    mass_out,
+    gather,
+    around,
     spack,
     south,
     scal,
-    out,
-    mass_out,
     recv,
     field,
     mass,
@@ -64,6 +73,7 @@
     lat_b = lat // devices
     per_row = LANES // lat_b
     wide = 3 * columns
+    total = columns * devices
 
     def remote(src, dst, send, recv_, to):
         return pltpu.make_async_remote_copy(
@@ -85,17 +95,6 @@
         )
     pl.semaphore_wait(barrier, devices - 1)
 
-    def field_copy(off):
-        to = lax.rem(me + off, devices)
-        return remote(spack.at[to], recv.at[me], f_send.at[off], f_recv.at[off], to)
-
-    def field_wait(off):
-        source = lax.rem(me + devices - off, devices)
-        return remote(spack.at[source], recv.at[source], f_send.at[off], f_recv.at[off], source)
-
-    for off in range(1, devices):
-        field_copy(off).start()
-
     def to_right(ch, phase):
         src, dst = (tin, hl1) if phase == 0 else (state, hl2)
         return remote(
@@ -111,6 +110,51 @@
     for ch in range(chunks):
         to_right(ch, 0).start()
         to_left(ch, 0).start()
+
+    def field_copy(off):
+        to = lax.rem(me + off, devices)
+        return remote(spack.at[to], recv.at[me], f_send.at[off], f_recv.at[off], to)
+
+    def field_wait(off):
+        source = lax.rem(me + devices - off, devices)
+        return remote(spack.at[source], recv.at[source], f_send.at[off], f_recv.at[off], source)
+
+    gather[...] = jnp.zeros_like(gather)
+    place = 0
+    for source in (air_in, east_in, north_in, up_in):
+        for l in range(source.shape[0]):
+            gather[place * lat_b : (place + 1) * lat_b, :total] = source[l]
+            place += 1
+    for h in range(FIELDS // per_row):
+        turned = gather[h * LANES : (h + 1) * LANES, :].T
+        around[h, 0:columns, :] = turned[total - columns : total]
+        around[h, columns : columns + total, :] = turned[:total]
+        around[h, columns + total : 2 * columns + total, :] = turned[:columns]
+    for to in range(devices):
+        for h in range(FIELDS // per_row):
+            spack[to, h, :wide, :] = around[h, to * columns : to * columns + wide, :]
+            spack[to, h, wide:, :] = jnp.ones((spack.shape[2] - wide, LANES), jnp.float32)
+
+    for off in range(1, devices):
+        field_copy(off).start()
+
+    counts = counts_in[...]
+    portion = 1.0 / counts.astype(jnp.float32)
+    for k in range(MAXSUB):
+        scal[k : k + 1, :] = jnp.where(k < counts, portion, 0.0)
+    for n in range(6):
+        scal[MAXSUB + n : MAXSUB + n + 1, :] = jnp.full(
+            (1, lat), flags_in[n].astype(jnp.float32), jnp.float32
+        )
+    tall = field.shape[1]
+    here = lax.broadcasted_iota(jnp.int32, (tall, total), 1)
+    want = lax.rem(
+        lax.broadcasted_iota(jnp.int32, (tall, total), 0) + me * columns + total - columns, total
+    )
+    for l in range(levels):
+        south[l] = jnp.sum(
+            jnp.where(here == want, south_in[l : l + 1, :], 0.0), axis=1, keepdims=True
+        )
 
     recv[me] = spack[me]
     for off in range(1, devices):
@@ -132,7 +176,7 @@
                         piece, lax.rem(lat_b * (place + per_row - g), LANES), 1
                     )
                     acc = jnp.where(lane // lat_b == place, turned, acc)
-                field[g * (FIELDS // per_row) + h, :, half * LANES : (half + 1) * LANES] = acc
+                field[h * per_row + g, :, half * LANES : (half + 1) * LANES] = acc
             return carry
 
         lax.fori_loop(0, per_row, unpack, 0)
@@ -143,8 +187,6 @@
     def second_order(flux, inv_up, number):
         size = jnp.abs(flux)
         return half_switch(number) * size * (1.0 - size * inv_up)
-
-    tall = field.shape[1]
 
     def x_air(l, base, number):
         m = mass[base, l]
@@ -351,11 +393,8 @@
     def stage_b(ch):
         across, carried = polar(ch, 0)
 
-        def level(l, carry):
+        for l in range(levels):
             y_level(ch, 0, 3, across, carried, l)
-            return carry
-
-        lax.fori_loop(0, levels, level, 0)
         acc = nothing
         for j in range(columns):
             c = columns + j
@@ -394,26 +433,23 @@
     def stage_c(ch):
         across, carried = polar(ch, 1)
 
-        def level(l, carry):
+        for l in range(levels):
             y_level(ch, 1, 6, across, carried, l)
-            return carry
-
-        lax.fori_loop(0, levels, level, 0)
         to_right(ch, 1).start()
         to_left(ch, 1).start()
 
     def step(i, carry):
+        @pl.when(i >= 2)
+        def _():
+            stage_c(i - 2)
+
+        @pl.when((i >= 1) & (i < chunks + 1))
+        def _():
+            stage_b(i - 1)
+
         @pl.when(i < chunks)
         def _():
             stage_a(i)
-
-        @pl.when((i >= 1) & (i < chunks + 1))
-        def _():
-            stage_b(i - 1)
-
-        @pl.when(i >= 2)
-        def _():
-            stage_c(i - 2)
 
         return carry
 
@@ -461,7 +497,6 @@
     substep_counts,
 ):
     devices = lax.axis_size("lon")
-    position = lax.axis_index("lon")
     count, levels, columns, lat = tracers.shape
     chunks = count // ROWS
     cells = levels * columns
@@ -476,26 +511,9 @@
     seeded = jnp.concatenate([surface[:, None], tracers[:, 1:]], axis=1)
     tin = seeded.reshape(chunks, ROWS, cells, lat).transpose(0, 2, 1, 3)
 
-    fields = jnp.concatenate([air_mass, east_flux, north_flux, upward_flux], axis=0)
-    fields = jnp.pad(fields, ((0, FIELDS - fields.shape[0]), (0, 0), (0, 0)))
-    bands = fields.reshape(per_row, folds, devices, columns, lat_b)
-    bands = bands.transpose(2, 1, 3, 0, 4).reshape(devices, folds, columns, LANES)
-    spack = jnp.concatenate([jnp.roll(bands, 1, 0), bands, jnp.roll(bands, -1, 0)], axis=2)
-    spack = jnp.pad(spack, ((0, 0), (0, 0), (0, tall - 3 * columns), (0, 0)))
-
-    doubled = jnp.concatenate([south_flux[:, -columns:], south_flux, south_flux[:, :tall]], axis=1)
-    south = lax.dynamic_slice_in_dim(doubled, position * columns, tall, 1)[:, :, None]
-
-    counts = substep_counts.astype(jnp.float32)
-    scal = jnp.concatenate(
-        [
-            jnp.where(
-                jnp.arange(MAXSUB)[:, None] < substep_counts[None], 1.0 / counts[None], 0.0
-            ),
-            jnp.broadcast_to(limiter_flags.astype(jnp.float32)[:, None], (6, lat)),
-        ],
-        axis=0,
-    )
+    turned = [x.transpose(0, 2, 1) for x in (air_mass, east_flux, north_flux, upward_flux)]
+    total = columns * devices
+    padded = -(-total // LANES) * LANES
 
     vmem = functools.partial(pltpu.VMEM, dtype=jnp.float32)
     band = (chunks, cells, ROWS, lat)
@@ -506,9 +524,15 @@
             jax.ShapeDtypeStruct(band, jnp.float32),
             jax.ShapeDtypeStruct((levels, columns, lat), jnp.float32),
         ),
-        in_specs=[pl.BlockSpec(memory_space=pltpu.VMEM)] * 4,
+        in_specs=[pl.BlockSpec(memory_space=pltpu.VMEM)] * 7
+        + [pl.BlockSpec(memory_space=pltpu.SMEM)],
         out_specs=[pl.BlockSpec(memory_space=pltpu.VMEM)] * 2,
         scratch_shapes=[
+            vmem((FIELDS * lat_b, padded)),
+            vmem((folds, -(-(total + 2 * columns) // 8) * 8, LANES)),
+            vmem((devices, folds, tall, LANES)),
+            vmem((levels, tall, 1)),
+            vmem((16, lat)),
             vmem((devices, folds, tall, LANES)),
             vmem((FIELDS, tall, lat)),
             vmem((11, levels, tall, lat)),
@@ -539,7 +563,7 @@
         compiler_params=pltpu.CompilerParams(
             collective_id=0, has_side_effects=True, vmem_limit_bytes=40 * 2**20
         ),
-    )(tin, spack, south, scal)
+    )(tin, *turned, south_flux, substep_counts[None], limiter_flags)
     transported = (
         out.reshape(chunks, cells, ROWS, lat)
         .transpose(0, 2, 1, 3)

time: 67 us -> 71.6 us (1.069)
  Pallas kernels: 56.3 us -> 65.2 us
  local copies, waits for them, and re-layouts: 8.32 us -> 5.29 us
  other arithmetic: 1.08 us -> 0.09 us
    pallas_call x1, Pallas kernels: 56.3 us -> 65.2 us  [per_device(): pl.pallas_call(functools.partial(kernel, devices, levels, columns, chunks...]
    unnamed x21, local copies, waits for them, and re-layouts: 4.85 us -> 2.91 us
    slice x11 -> x0, local copies, waits for them, and re-layouts: 1.22 us -> none  [the longest x6 0.77 us: per_device(): jnp.roll(bands, 1, 0)]
    slice x1, local copies, waits for them, and re-layouts: 0.2 us -> 1.34 us  [per_device(): seeded = jnp.concatenate([surface[:, None], tracers[:, 1:]], axis=1)]
    concatenate x4 -> x0, other arithmetic: 0.98 us -> none  [the longest x1 0.75 us: per_device(): jnp.concatenate([air_mass, east_flux, north_flux, upward_flux], axis=0)]
where the time goes in v1:
time: 71.6 us; the launch traced here: 71.4 us
  Pallas kernels  65.2 us (91%)
  local copies, waits for them, and re-layouts  5.29 us (7%)
  between operations  0.76 us (1%)
    pallas_call x1, Pallas kernels, per_device(): pl.pallas_call(functools.partial(kernel, devices, levels, columns, chunks...  65.2 us
    unnamed x21, local copies, waits for them, and re-layouts  2.91 us

profile of v1, /device:TPU:1, one launch (start us, length us, event | category | flops | bytes accessed | tf_op | source)
XLA Modules:
  0.0 71.4 jit_solution(2971104164996328981)
XLA Ops:
  0.6 0.0 slice-start
  0.6 0.0 copy-start.7
  0.7 0.0 copy-start.8
  0.7 0.9 %slice-done = f32[32,1,6,256]{3,1,2,0:T(1,128)S(1)} async-done(((f32[32,4,6,256]{3,1,2,0:T(4,128)}), f32[32,1,6,256]{3,1,2,0:T(1,128)S(1)}, s32[]{:S(2)}) %slice-start) | async-done | bytes 196632 | tf_op jit(solution)/shard_map/slice | solution.py:510
  1.6 0.0 copy-done.7
  1.6 0.0 copy-done.8
  1.6 1.3 %slice.7 = f32[32,3,6,256]{3,1,2,0:T(4,128)S(1)} slice(f32[32,4,6,256]{3,1,2,0:T(4,128)} %param.10), slice={[0:32], [1:4], [0:6], [0:256]} | slice | bytes 1179648 | tf_op jit(solution)/shard_map/slice | solution.py:511
  2.9 0.2 copy.20
  3.1 0.1 pad_maximum_fusion
  3.2 0.0 copy-start
  3.2 0.0 copy-start.1
  3.2 0.0 copy-start.2
  3.3 0.0 copy-start.3
  3.3 0.0 copy-start.4
  3.3 0.1 copy.23
  3.3 0.0 copy-start.5
  3.4 0.0 copy-start.6
  3.4 0.6 copy-done
  4.0 0.0 copy-done.1
  4.0 0.0 copy-done.2
  4.0 0.0 copy-done.3
  4.0 0.0 copy-done.4
  4.0 0.0 copy-done.5
  4.0 0.0 copy-done.6
  4.0 65.2 %shard_map.113 = (f32[4,24,8,256]{3,2,1,0:T(8,128)S(1)}, f32[4,6,256]{2,1,0:T(8,128)S(1)}) custom-call(f32[4,24,8,256]{3,2,1,0:T(8,128)S(1)} %bitcast.11, f32[4,16,96]{2,1,0:T(8,128)S(1)} %bitcast.13, f32[4,16,96]{2,1,0:T(8,128)S(1)} %bitcast.14, f32[4,16,96]{2,1,0:T(8,128)S(1)} %bitcast.15, f32[3,16,96]{2,1,0:T(8,128)S(1)} %bitcast.16, ...), custom_call_target="tpu_custom_call" | custom-call | tf_op jit(solution)/shard_map/pallas_call | solution.py:521
  69.3 0.1 copy.16
  69.4 1.4 %copy.17 = f32[32,4,6,256]{3,1,2,0:T(4,128)} copy(f32[32,4,6,256]{3,0,2,1:T(8,128)S(1)} %bitcast.19) | data formatting | bytes 1572864
  70.8 0.6 copy.18
  (1 shorter events, 0.0 us)
Async XLA Ops:
  0.6 0.9 %slice-start = ((f32[32,4,6,256]{3,1,2,0:T(4,128)}), f32[32,1,6,256]{3,1,2,0:T(1,128)S(1)}, s32[]{:S(2)}) async-start(f32[32,4,6,256]{3,1,2,0:T(4,128)} %param.10), calls=%async_computation | async-start | bytes 393216 | tf_op jit(solution)/shard_map/slice | solution.py:510
  0.6 0.9 %copy-start.7 = (f32[6,256]{1,0:T(8,128)S(1)}, f32[6,256]{1,0:T(8,128)}, u32[]{:S(2)}) copy-start(f32[6,256]{1,0:T(8,128)} %param.16) | copy-start | bytes 18436
  0.7 0.9 %copy-start.8 = (s32[6,256]{1,0:T(8,128)S(1)}, s32[6,256]{1,0:T(8,128)}, u32[]{:S(2)}) copy-start(s32[6,256]{1,0:T(8,128)} %param.17) | copy-start | bytes 18436
  3.2 0.8 %copy-start = (f32[4,96,16]{1,2,0:T(8,128)S(1)}, f32[4,96,16]{1,2,0:T(8,128)}, u32[]{:S(2)}) copy-start(f32[4,96,16]{1,2,0:T(8,128)} %param.11) | copy-start | bytes 73732
  3.2 0.8 %copy-start.1 = (f32[4,96,16]{1,2,0:T(8,128)S(1)}, f32[4,96,16]{1,2,0:T(8,128)}, u32[]{:S(2)}) copy-start(f32[4,96,16]{1,2,0:T(8,128)} %param.12) | copy-start | bytes 73732
  3.2 0.8 %copy-start.2 = (f32[4,96,16]{1,2,0:T(8,128)S(1)}, f32[4,96,16]{1,2,0:T(8,128)}, u32[]{:S(2)}) copy-start(f32[4,96,16]{1,2,0:T(8,128)} %param.13) | copy-start | bytes 73732
  3.3 0.8 %copy-start.3 = (f32[3,96,16]{1,2,0:T(8,128)S(1)}, f32[3,96,16]{1,2,0:T(8,128)}, u32[]{:S(2)}) copy-start(f32[3,96,16]{1,2,0:T(8,128)} %param.15) | copy-start | bytes 55300
  3.3 0.8 %copy-start.4 = (f32[4,96]{1,0:T(4,128)S(1)}, f32[4,96]{1,0:T(4,128)}, u32[]{:S(2)}) copy-start(f32[4,96]{1,0:T(4,128)} %south_in.1) | copy-start | bytes 4612
  3.3 0.7 copy-start.5
  3.4 0.7 copy-start.6

commit v2 on v1

--- a/solution.py
+++ b/solution.py
@@ -8,6 +8,7 @@
 from jax.sharding import PartitionSpec as P
 
 MAXSUB = 3
+AHEAD = 2
 ROWS = 8
 LANES = 128
 FIELDS = 16
@@ -107,10 +108,6 @@
             src.at[ch], dst.at[ch], h_send.at[phase, 1, ch], h_recv.at[phase, 1, ch], left
         )
 
-    for ch in range(chunks):
-        to_right(ch, 0).start()
-        to_left(ch, 0).start()
-
     def field_copy(off):
         to = lax.rem(me + off, devices)
         return remote(spack.at[to], recv.at[me], f_send.at[off], f_recv.at[off], to)
@@ -137,6 +134,9 @@
 
     for off in range(1, devices):
         field_copy(off).start()
+    for ch in range(1):
+        to_right(ch, 0).start()
+        to_left(ch, 0).start()
 
     counts = counts_in[...]
     portion = 1.0 / counts.astype(jnp.float32)
@@ -159,6 +159,9 @@
     recv[me] = spack[me]
     for off in range(1, devices):
         field_wait(off).wait_recv()
+    for ch in range(1, AHEAD):
+        to_right(ch, 0).start()
+        to_left(ch, 0).start()
 
     lane = lax.broadcasted_iota(jnp.int32, (1, LANES), 1)
     lane_lat = lax.broadcasted_iota(jnp.int32, (1, lat), 1)
@@ -439,17 +442,22 @@
         to_left(ch, 1).start()
 
     def step(i, carry):
+        @pl.when((i >= 1) & (i < chunks + 1))
+        def _():
+            stage_b(i - 1)
+
+        @pl.when(i < chunks)
+        def _():
+            stage_a(i)
+
+        @pl.when(i < chunks - AHEAD)
+        def _():
+            to_right(i + AHEAD, 0).start()
+            to_left(i + AHEAD, 0).start()
+
         @pl.when(i >= 2)
         def _():
             stage_c(i - 2)
-
-        @pl.when((i >= 1) & (i < chunks + 1))
-        def _():
-            stage_b(i - 1)
-
-        @pl.when(i < chunks)
-        def _():
-            stage_a(i)
 
         return carry
 

time: 71.6 us -> 61.1 us (0.85)
  Pallas kernels: 65.2 us -> 54.7 us
    pallas_call x1, Pallas kernels: 65.2 us -> 54.7 us  [per_device(): pl.pallas_call(functools.partial(kernel, devices, levels, columns, chunks...]
where the time goes in v2:
time: 61.1 us; the launch traced here: 60.9 us
  Pallas kernels  54.7 us (90%)
  local copies, waits for them, and re-layouts  5.29 us (9%)
  between operations  0.76 us (1%)
    pallas_call x1, Pallas kernels, per_device(): pl.pallas_call(functools.partial(kernel, devices, levels, columns, chunks...  54.7 us
    unnamed x21, local copies, waits for them, and re-layouts  2.91 us
    slice x1, local copies, waits for them, and re-layouts, per_device(): seeded = jnp.concatenate([surface[:, None], tracers[:, 1:]], axis=1)  1.34 us

profile of v2, /device:TPU:1, one launch (start us, length us, event | category | flops | bytes accessed | tf_op | source)
XLA Modules:
  0.0 60.9 jit_solution(15815909019724408121)
XLA Ops:
  0.6 0.0 slice-start
  0.6 0.0 copy-start.7
  0.7 0.0 copy-start.8
  0.7 0.9 %slice-done = f32[32,1,6,256]{3,1,2,0:T(1,128)S(1)} async-done(((f32[32,4,6,256]{3,1,2,0:T(4,128)}), f32[32,1,6,256]{3,1,2,0:T(1,128)S(1)}, s32[]{:S(2)}) %slice-start) | async-done | bytes 196632 | tf_op jit(solution)/shard_map/slice | solution.py:518
  1.6 0.0 copy-done.7
  1.6 0.0 copy-done.8
  1.6 1.3 %slice.7 = f32[32,3,6,256]{3,1,2,0:T(4,128)S(1)} slice(f32[32,4,6,256]{3,1,2,0:T(4,128)} %param.10), slice={[0:32], [1:4], [0:6], [0:256]} | slice | bytes 1179648 | tf_op jit(solution)/shard_map/slice | solution.py:519
  2.9 0.2 copy.20
  3.1 0.1 pad_maximum_fusion
  3.2 0.0 copy-start
  3.2 0.0 copy-start.1
  3.2 0.0 copy-start.2
  3.3 0.0 copy-start.3
  3.3 0.0 copy-start.4
  3.3 0.1 copy.23
  3.3 0.0 copy-start.5
  3.4 0.0 copy-start.6
  3.4 0.6 copy-done
  4.0 0.0 copy-done.1
  4.0 0.0 copy-done.2
  4.0 0.0 copy-done.3
  4.0 0.0 copy-done.4
  4.0 0.0 copy-done.5
  4.0 0.0 copy-done.6
  4.0 54.7 %shard_map.113 = (f32[4,24,8,256]{3,2,1,0:T(8,128)S(1)}, f32[4,6,256]{2,1,0:T(8,128)S(1)}) custom-call(f32[4,24,8,256]{3,2,1,0:T(8,128)S(1)} %bitcast.11, f32[4,16,96]{2,1,0:T(8,128)S(1)} %bitcast.13, f32[4,16,96]{2,1,0:T(8,128)S(1)} %bitcast.14, f32[4,16,96]{2,1,0:T(8,128)S(1)} %bitcast.15, f32[3,16,96]{2,1,0:T(8,128)S(1)} %bitcast.16, ...), custom_call_target="tpu_custom_call" | custom-call | tf_op jit(solution)/shard_map/pallas_call | solution.py:529
  58.8 0.1 copy.16
  58.9 1.4 %copy.17 = f32[32,4,6,256]{3,1,2,0:T(4,128)} copy(f32[32,4,6,256]{3,0,2,1:T(8,128)S(1)} %bitcast.19) | data formatting | bytes 1572864
  60.3 0.6 %copy.18 = f32[4,6,256]{2,0,1:T(4,128)} copy(f32[4,6,256]{2,1,0:T(8,128)S(1)} %get-tuple-element.9) | data formatting | bytes 49152
  (1 shorter events, 0.0 us)
Async XLA Ops:
  0.6 0.9 %slice-start = ((f32[32,4,6,256]{3,1,2,0:T(4,128)}), f32[32,1,6,256]{3,1,2,0:T(1,128)S(1)}, s32[]{:S(2)}) async-start(f32[32,4,6,256]{3,1,2,0:T(4,128)} %param.10), calls=%async_computation | async-start | bytes 393216 | tf_op jit(solution)/shard_map/slice | solution.py:518
  0.6 0.9 %copy-start.7 = (f32[6,256]{1,0:T(8,128)S(1)}, f32[6,256]{1,0:T(8,128)}, u32[]{:S(2)}) copy-start(f32[6,256]{1,0:T(8,128)} %param.16) | copy-start | bytes 18436
  0.7 0.9 %copy-start.8 = (s32[6,256]{1,0:T(8,128)S(1)}, s32[6,256]{1,0:T(8,128)}, u32[]{:S(2)}) copy-start(s32[6,256]{1,0:T(8,128)} %param.17) | copy-start | bytes 18436
  3.2 0.8 %copy-start = (f32[4,96,16]{1,2,0:T(8,128)S(1)}, f32[4,96,16]{1,2,0:T(8,128)}, u32[]{:S(2)}) copy-start(f32[4,96,16]{1,2,0:T(8,128)} %param.11) | copy-start | bytes 73732
  3.2 0.8 %copy-start.1 = (f32[4,96,16]{1,2,0:T(8,128)S(1)}, f32[4,96,16]{1,2,0:T(8,128)}, u32[]{:S(2)}) copy-start(f32[4,96,16]{1,2,0:T(8,128)} %param.12) | copy-start | bytes 73732
  3.2 0.8 %copy-start.2 = (f32[4,96,16]{1,2,0:T(8,128)S(1)}, f32[4,96,16]{1,2,0:T(8,128)}, u32[]{:S(2)}) copy-start(f32[4,96,16]{1,2,0:T(8,128)} %param.13) | copy-start | bytes 73732
  3.3 0.8 %copy-start.3 = (f32[3,96,16]{1,2,0:T(8,128)S(1)}, f32[3,96,16]{1,2,0:T(8,128)}, u32[]{:S(2)}) copy-start(f32[3,96,16]{1,2,0:T(8,128)} %param.15) | copy-start | bytes 55300
  3.3 0.8 %copy-start.4 = (f32[4,96]{1,0:T(4,128)S(1)}, f32[4,96]{1,0:T(4,128)}, u32[]{:S(2)}) copy-start(f32[4,96]{1,0:T(4,128)} %south_in.1) | copy-start | bytes 4612
  3.3 0.7 %copy-start.5 = (s32[256]{0:T(256)S(1)}, s32[256]{0:T(256)}, u32[]{:S(2)}) copy-start(s32[256]{0:T(256)} %param.19) | copy-start | bytes 3076
  3.4 0.7 %copy-start.6 = (s32[6]{0:T(128)S(1)}, s32[6]{0:T(128)}, u32[]{:S(2)}) copy-start(s32[6]{0:T(128)} %flags_in.1) | copy-start | bytes 76
